TPU v7x, 32 devices: a whole 2x2x4 slice. The times are simulated.
32 devices in a mesh: loop: 4 (over y, x), group: 8 (over z, core).
Axes of the slice: x: 2, y: 2, z: 4, core: 2. Of those that a mesh axis runs over, the one named last changes fastest.
Arguments:
- view_embeds: bfloat16 [32768, 1152], P(('loop', 'group')), may hold values from -0.1875 to 0.1875
- view_image: int32 [32768], P(('loop', 'group')), may hold values from 0 to 8191, as said below
- view_counts: int32 [8192], P(('loop', 'group')), may hold values from 2 to 6, as said below
- text_feats: bfloat16 [8192, 1152], P(('loop', 'group')), may hold values from -0.1875 to 0.1875
- head_weight: bfloat16 [1152, 1152], replicated, may hold values from -0.1875 to 0.1875
- logit_scale: float32 [1], replicated, may hold values from 5 to 15
- logit_bias: float32 [1], replicated, may hold values from -3 to -1
Outputs:
- view_grad: bfloat16 [32768, 1152], P(('loop', 'group'))
- view_loss: bfloat16 [32768], P(('loop', 'group'))
- text_grad: bfloat16 [8192, 1152], P(('loop', 'group'))
- head_grad: float32 [1152, 1152], P('group')
Inputs may be any that keep to these rules, and one draw needn't show every extreme that they name: view_counts[i] is the number of rows of view_image that name image i. `view_image`: the 1024 rows of one device name only images whose captions lie on a device with the same loop index. At most 176 of one device's rows name images held by any one device, and in every draw some devices hold images named by exactly 176 rows of every device with their loop index. The images of one loss group have 4096 view rows in all.
All inputs are finite; a program needn't handle non-finite values.
Results may differ from a plain program's by a relative error of at most 0.015.
Values may be sent and summed in bfloat16 or wider, within the bound.
No kernel may reach another device: no remote copies, remote signals or barrier semaphores. Data moves between devices by JAX's collectives and lax.ppermute only.
A program may use at most 128 MiB of HBM per device.

v0:
```python
import jax
import jax.numpy as jnp
from jax import lax
from jax.sharding import PartitionSpec as P

epsilon = 1e-06


def unit_rows(values):
    inverse = lax.rsqrt(jnp.sum(values * values, axis=1, keepdims=True) + epsilon)
    return (values * inverse, inverse)


def local(view_embeds, view_image, view_counts, text_feats, head_weight, logit_scale, logit_bias):
    per_device = view_counts.shape[0]
    feature_width = view_embeds.shape[1]
    group_size = lax.axis_size("group")
    loop_size = lax.axis_size("loop")
    slot_count = 11 * per_device // (2 * group_size)
    group_caps = per_device * loop_size
    target_group = view_image // per_device % group_size
    local_image = view_image % per_device
    chosen = (target_group[:, None] == jnp.arange(group_size, dtype=jnp.int32)[None, :]).astype(
        jnp.int32
    )
    earlier = jnp.cumsum(chosen, axis=0) - chosen
    slot_place = target_group * slot_count + jnp.sum(earlier * chosen, axis=1)
    send_rows = (
        jnp.zeros((group_size * slot_count, feature_width), jnp.bfloat16)
        .at[slot_place]
        .set(view_embeds)
    )
    send_ids = jnp.full((group_size * slot_count,), -1, jnp.int32).at[slot_place].set(local_image)
    held_rows, held_ids = (
        lax.all_to_all(send_rows, "group", split_axis=0, concat_axis=0, tiled=True),
        lax.all_to_all(send_ids, "group", split_axis=0, concat_axis=0, tiled=True),
    )
    x_unit, inv_x = unit_rows(held_rows.astype(jnp.float32))
    x_half = x_unit.astype(jnp.bfloat16)
    inv_count = 1.0 / view_counts.astype(jnp.float32)
    matches = held_ids[:, None] == jnp.arange(per_device, dtype=jnp.int32)[None, :]
    row_weight = jnp.sum(jnp.where(matches, inv_count[None, :], 0.0), axis=1)
    text_embed = jnp.dot(text_feats, head_weight, preferred_element_type=jnp.float32)
    y_unit, inv_y = unit_rows(text_embed)
    y_half = y_unit.astype(jnp.bfloat16)
    loop_index = lax.axis_index("loop")
    positive_column = loop_index * per_device + held_ids
    logit_mult = logit_scale[0]
    offset = logit_bias[0]
    captions = lax.all_gather(y_half, "loop", axis=0, tiled=True)
    scores = jnp.einsum("rd,cd->rc", x_half, captions, preferred_element_type=jnp.float32)
    columns = jnp.arange(captions.shape[0], dtype=jnp.int32)
    labels = jnp.where(positive_column[:, None] == columns[None, :], 1.0, -1.0)
    margin = -labels * (logit_mult * scores + offset)
    loss_part = jnp.sum(jax.nn.softplus(margin), axis=1)
    pair_grad = (row_weight[:, None] * logit_mult * -labels * jax.nn.sigmoid(margin)).astype(
        jnp.bfloat16
    )
    loss_part, pair_grad = (loss_part, pair_grad)
    grad_sum = jnp.dot(pair_grad, captions, preferred_element_type=jnp.float32)
    add_kept_tiles = pair_grad
    grad_sum, loss_sum, kept_tiles = (grad_sum, loss_part, add_kept_tiles)
    pair_grad = kept_tiles
    gy_unit = lax.psum_scatter(
        jnp.einsum("rc,rd->cd", pair_grad, x_half, preferred_element_type=jnp.float32),
        "loop",
        scatter_dimension=0,
        tiled=True,
    )
    view_part = (grad_sum - x_unit * jnp.sum(x_unit * grad_sum, axis=1, keepdims=True)) * inv_x
    loss_half = (loss_sum / group_caps).astype(jnp.bfloat16)
    back_rows, back_loss = (
        lax.all_to_all(
            view_part.astype(jnp.bfloat16), "group", split_axis=0, concat_axis=0, tiled=True
        ),
        lax.all_to_all(loss_half, "group", split_axis=0, concat_axis=0, tiled=True),
    )
    view_grad = back_rows[slot_place]
    view_loss = back_loss[slot_place]
    caption_grad = (gy_unit - y_unit * jnp.sum(y_unit * gy_unit, axis=1, keepdims=True)) * inv_y
    grad_half = caption_grad.astype(jnp.bfloat16)
    text_grad = jnp.einsum(
        "cd,ed->ce", grad_half, head_weight, preferred_element_type=jnp.float32
    ).astype(jnp.bfloat16)
    head_share = lax.psum_scatter(
        jnp.einsum("cd,ce->de", text_feats, grad_half, preferred_element_type=jnp.float32).astype(
            jnp.bfloat16
        ),
        "group",
        scatter_dimension=0,
        tiled=True,
    )
    head_grad = lax.psum(head_share, "loop").astype(jnp.float32)
    return (view_grad, view_loss, text_grad, head_grad)


def solution(mesh):
    return jax.shard_map(
        local,
        mesh=mesh,
        in_specs=(
            P(("loop", "group"), None),
            P(("loop", "group")),
            P(("loop", "group")),
            P(("loop", "group"), None),
            P(),
            P(),
            P(),
        ),
        out_specs=(
            P(("loop", "group"), None),
            P(("loop", "group")),
            P(("loop", "group"), None),
            P("group", None),
        ),
        check_vma=False,
    )
```

profile of v0, /device:TPU:0, one launch (start us, length us, event | category | flops | bytes accessed | tf_op | source)
XLA Modules:
  0.0 352.3 jit_solution(10495240025333414487)
XLA Ops:
  7.2 0.0 copy-start
  7.2 0.9 add_select_fusion
  8.0 2.3 reduce-window.6
  10.3 0.3 slice_reduce_fusion
  10.6 0.2 reduce-window.9
  10.8 0.1 add_bitcast_fusion
  10.9 4.3 %scatter_custom_fusion = s32[1408]{0:T(1024)S(1)} fusion(s32[1024]{0:T(1024)S(1)} %get-tuple-element.21, s32[1024]{0:T(1024)S(1)} %get-tuple-element.24, s32[]{:T(128)} %constant.56.clone.1), kind=kCustom, calls=%fused_computation.50 | custom fusion | bytes 5636 | tf_op jit(solution)/shard_map/scatter | solution.py:33
  15.2 0.7 all_to_all.35
  15.9 6.3 %all-to-all-start = ((s32[8,176,1]{1,2,0:T(1,128)}), s32[8,176,1]{1,2,0:T(1,128)S(1)}, u32[]{:S(2)}, u32[]{:S(2)}) async-start(s32[8,176,1]{1,2,0:T(1,128)} %all_to_all.35), calls=%async_computation | async-start | bytes 16384 | tf_op jit(solution)/shard_map/all_to_all | solution.py:36
  22.2 8.2 %scatter_custom_fusion.1 = bf16[1408,1152]{1,0:T(8,128)(2,1)} fusion(s32[1024]{0:T(1024)S(1)} %get-tuple-element.21, bf16[1024,1152]{1,0:T(8,128)(2,1)} %param.7, bf16[]{:T(256)} %constant.69.clone.1), kind=kCustom, calls=%fused_computation.18 | custom fusion | bytes 3244544 | tf_op jit(solution)/shard_map/scatter | solution.py:31
  30.4 0.0 all-to-all-done
  30.4 0.0 copy-start.3
  30.4 5.2 %all-to-all-start.1 = ((bf16[8,176,1152]{2,1,0:T(8,128)(2,1)}), bf16[8,176,1152]{2,1,0:T(8,128)(2,1)}, u32[]{:S(2)}, u32[]{:S(2)}) async-start(bf16[8,176,1152]{2,1,0:T(8,128)(2,1)} %bitcast.54), calls=%async_computation.1 | async-start | bytes 6488064 | tf_op jit(solution)/shard_map/all_to_all | solution.py:35
  35.6 0.0 copy-start.4
  35.6 0.0 all-gather.2.cloned.1.call-start
  35.7 0.0 copy-done
  35.7 0.0 copy-done.3
  35.7 1.1 multiply_reduce_fusion.3
  36.8 0.0 copy-start.1
  36.8 1.0 copy-done.1
  37.8 0.9 multiply_convert_fusion.3
  38.8 0.0 all-gather.2.cloned.1.call-update
  38.8 0.2 reduce-scatter.5.cloned.1.call-start
  40.3 0.0 copy-done.4
  40.4 0.1 eq.61
  40.5 0.5 select_reduce_fusion
  41.0 68.4 %all-to-all-done.1 = bf16[8,176,1152]{2,1,0:T(8,128)(2,1)} async-done(((bf16[8,176,1152]{2,1,0:T(8,128)(2,1)}), bf16[8,176,1152]{2,1,0:T(8,128)(2,1)}, u32[]{:S(2)}, u32[]{:S(2)}) %all-to-all-start.1) | async-done | bytes 3244064 | tf_op jit(solution)/shard_map/all_to_all | solution.py:35
  109.4 2.6 multiply_reduce_fusion.1
  112.0 0.1 rsqrt.20
  112.1 4.2 %fusion.2 = bf16[1408,1152]{1,0:T(8,128)(2,1)} fusion(bf16[8,176,1152]{2,1,0:T(8,128)(2,1)} %all-to-all-done.1, f32[1408]{0:T(1024)S(1)} %rsqrt.20), kind=kLoop, calls=%fused_computation.16 | loop fusion | flops 4866048 | bytes 6493696 | tf_op jit(solution)/shard_map/convert_element_type | solution.py:39
  116.3 0.0 all-gather.2.cloned.1.call-done
  116.3 0.0 copy-start.2
  116.3 11.6 %fusion.1 = (f32[1408]{0:T(1024)S(1)}, bf16[1408,1024]{0,1:T(8,128)(2,1)S(1)}) fusion(s32[1408]{0:T(1024)S(1)} %broadcast_add_fusion, f32[1408]{0:T(1024)S(1)} %broadcast_multiply_fusion, f32[]{:T(128)} %bitcast.50, bf16[1408,1152]{1,0:T(8,128)(2,1)} %fusion.2, bf16[1024,1152]{1,0:T(8,128)(2,1)} %all-gather.2.cloned.1.call-done, f32[]{:T(128)} %bitcast.49), kind=kOutput, calls=%fused_computation.11 | convolution fusion | flops 3349281280 | bytes 8503816 | tf_op jit(solution)/shard_map/rd,cd->rc/dot_general | solution.py:51
  127.9 0.0 copy-start.5
  127.9 1.6 copy-done.5
  129.5 0.0 copy-done.2
  129.5 5.7 %fusion.14 = f32[1024,1152]{1,0:T(8,128)} fusion(bf16[1408,1024]{0,1:T(8,128)(2,1)S(1)} %get-tuple-element.23, bf16[1408,1152]{1,0:T(8,128)(2,1)S(1)} %copy-done.2), kind=kOutput, calls=%fused_computation.57 | convolution fusion | flops 3321888768 | bytes 10846208 | tf_op jit(solution)/shard_map/rc,rd->cd/dot_general | solution.py:65
  135.3 0.0 reduce-scatter.5.cloned.1.call-update
  135.3 0.7 convert_element_type.77
  136.0 3.6 %all-to-all-start.3 = ((bf16[8,176,1]{1,2,0:T(2,128)(2,1)}), bf16[8,176,1]{1,2,0:T(2,128)(2,1)S(1)}, u32[]{:S(2)}, u32[]{:S(2)}) async-start(bf16[8,176,1]{1,2,0:T(2,128)(2,1)} %convert_element_type.77), calls=%async_computation.3 | async-start | bytes 16384 | tf_op jit(solution)/shard_map/all_to_all | solution.py:76
  139.6 8.4 %multiply_reduce_fusion = (f32[1408]{0:T(1024)S(1)}, f32[1408,1152]{1,0:T(8,128)S(1)}) fusion(bf16[8,176,1152]{2,1,0:T(8,128)(2,1)} %all-to-all-done.1, f32[1408]{0:T(1024)S(1)} %rsqrt.20, bf16[1408,1024]{0,1:T(8,128)(2,1)} %copy-done.5, bf16[1024,1152]{1,0:T(8,128)(2,1)} %all-gather.2.cloned.1.call-done), kind=kOutput, calls=%fused_computation.9 | convolution fusion | flops 3328375296 | bytes 14986240 | tf_op jit(solution)/shard_map/dot_general | solution.py:60
  148.0 4.0 %multiply_convert_fusion = bf16[1408,1152]{1,0:T(8,128)(2,1)} fusion(f32[1408,1152]{1,0:T(8,128)S(1)} %get-tuple-element.29, bf16[8,176,1152]{2,1,0:T(8,128)(2,1)} %all-to-all-done.1, f32[1408]{0:T(1024)S(1)} %get-tuple-element.28, f32[1408]{0:T(1024)S(1)} %rsqrt.20), kind=kLoop, calls=%fused_computation.8 | loop fusion | flops 9732096 | bytes 12987392 | tf_op jit(solution)/shard_map/convert_element_type | solution.py:74
  152.0 39.5 %reduce-scatter.5.cloned.1.call-done = f32[256,1152]{1,0:T(8,128)} async-done(((f32[1024,1152]{1,0:T(8,128)}), f32[256,1152]{1,0:T(8,128)}) %reduce-scatter.5.cloned.1.call-update) | async-done | bytes 1179664 | tf_op jit(solution)/shard_map/reduce_scatter | solution.py:64
  191.5 1.9 multiply_reduce_fusion.2
  193.3 0.0 all-to-all-done.3
  193.4 4.6 %all-to-all-start.2 = ((bf16[8,176,1152]{2,1,0:T(8,128)(2,1)}), bf16[8,176,1152]{2,1,0:T(8,128)(2,1)}, u32[]{:S(2)}, u32[]{:S(2)}) async-start(bf16[8,176,1152]{2,1,0:T(8,128)(2,1)} %bitcast.53), calls=%async_computation.2 | async-start | bytes 6488064 | tf_op jit(solution)/shard_map/all_to_all | solution.py:73
  198.0 0.0 reduce-scatter.7.cloned.1.call-start
  198.0 1.9 multiply_convert_fusion.2
  199.9 3.6 %fusion = bf16[1152,1152]{0,1:T(8,128)(2,1)} fusion(bf16[256,1152]{1,0:T(8,128)(2,1)S(1)} %multiply_convert_fusion.2, bf16[256,1152]{1,0:T(8,128)(2,1)} %param.10), kind=kOutput, calls=%fused_computation.6 | convolution fusion | flops 680804352 | bytes 3833856 | tf_op jit(solution)/shard_map/cd,ce->de/dot_general | solution.py:86
  203.5 5.2 %copy.19 = bf16[1152,1152]{1,0:T(8,128)(2,1)} copy(bf16[1152,1152]{0,1:T(8,128)(2,1)} %fusion) | data formatting | bytes 5308416
  208.7 0.0 reduce-scatter.7.cloned.1.call-update
  208.7 0.0 all-reduce.2.cloned.1.call-start
  208.8 77.4 %reduce-scatter.7.cloned.1.call-done = bf16[144,1152]{1,0:T(8,128)(2,1)} async-done(((bf16[1152,1152]{1,0:T(8,128)(2,1)}), bf16[144,1152]{1,0:T(8,128)(2,1)}) %reduce-scatter.7.cloned.1.call-update) | async-done | bytes 331792
  286.2 2.0 copy.20
  288.2 0.0 all-reduce.2.cloned.1.call-update
  288.3 0.1 all_to_all.34
  288.4 11.3 %gather_fusion.1 = bf16[1024]{0:T(1024)(128)(2,1)} fusion(bf16[1408]{0:T(1024)(128)(2,1)S(1)} %all_to_all.34, s32[1024]{0:T(1024)S(1)} %get-tuple-element.20), kind=kCustom, calls=%fused_computation.1 | custom fusion | bytes 8192 | tf_op jit(solution)/shard_map/gather | solution.py:79
  299.7 0.0 all-to-all-done.2
  299.7 8.7 %gather_fusion = bf16[1024,1152]{1,0:T(8,128)(2,1)} fusion(bf16[1408,1152]{1,0:T(8,128)(2,1)} %bitcast.7, s32[1024]{0:T(1024)S(1)} %get-tuple-element.20), kind=kCustom, calls=%fused_computation | custom fusion | bytes 4722688 | tf_op jit(solution)/shard_map/gather | solution.py:78
  308.4 1.9 convolution_convert_fusion.1
  310.3 33.4 %all-reduce.2.cloned.1.call-done = bf16[144,1152]{0,1:T(8,128)(2,1)} async-done(((bf16[144,1152]{0,1:T(8,128)(2,1)}), bf16[144,1152]{0,1:T(8,128)(2,1)}) %all-reduce.2.cloned.1.call-update) | async-done | bytes 331792 | tf_op jit(solution)/shard_map/psum | solution.py:93
  343.7 2.1 copy.18
  (11 shorter events, 0.1 us)
Async XLA Ops:
  7.2 28.5 %copy-start = (bf16[1152,1152]{1,0:T(8,128)(2,1)S(1)}, bf16[1152,1152]{1,0:T(8,128)(2,1)}, u32[]{:S(2)}) copy-start(bf16[1152,1152]{1,0:T(8,128)(2,1)} %param.11) | copy-start | bytes 7962628
  15.9 14.5 %all-to-all-start = ((s32[8,176,1]{1,2,0:T(1,128)}), s32[8,176,1]{1,2,0:T(1,128)S(1)}, u32[]{:S(2)}, u32[]{:S(2)}) async-start(s32[8,176,1]{1,2,0:T(1,128)} %all_to_all.35), calls=%async_computation | async-start | bytes 16384 | tf_op jit(solution)/shard_map/all_to_all | solution.py:36
  30.4 5.3 %copy-start.3 = (bf16[256,1152]{1,0:T(8,128)(2,1)S(1)}, bf16[256,1152]{1,0:T(8,128)(2,1)}, u32[]{:S(2)}) copy-start(bf16[256,1152]{1,0:T(8,128)(2,1)} %param.10) | copy-start | bytes 1769476
  30.4 79.0 %all-to-all-start.1 = ((bf16[8,176,1152]{2,1,0:T(8,128)(2,1)}), bf16[8,176,1152]{2,1,0:T(8,128)(2,1)}, u32[]{:S(2)}, u32[]{:S(2)}) async-start(bf16[8,176,1152]{2,1,0:T(8,128)(2,1)} %bitcast.54), calls=%async_computation.1 | async-start | bytes 6488064 | tf_op jit(solution)/shard_map/all_to_all | solution.py:35
  35.6 4.7 %copy-start.4 = (s32[256]{0:T(256)S(1)}, s32[256]{0:T(256)}, u32[]{:S(2)}) copy-start(s32[256]{0:T(256)} %param.9) | copy-start | bytes 3076
  35.6 80.7 %all-gather.2.cloned.1.call-start = ((), (), s32[]{:S(2)}) async-start(), calls=%async_computation.6 | async-start | bytes 2949120 | tf_op jit(solution)/shard_map/all_gather | solution.py:50
  36.8 1.0 copy-start.1
  38.8 152.7 %reduce-scatter.5.cloned.1.call-start = ((), (), s32[]{:S(2)}) async-start(), calls=%async_computation.7 | async-start | bytes 5898240 | tf_op jit(solution)/shard_map/reduce_scatter | solution.py:64
  116.3 13.2 %copy-start.2 = (bf16[1408,1152]{1,0:T(8,128)(2,1)S(1)}, bf16[1408,1152]{1,0:T(8,128)(2,1)}, u32[]{:S(2)}) copy-start(bf16[1408,1152]{1,0:T(8,128)(2,1)} %fusion.2) | copy-start | bytes 9732100
  127.9 1.6 copy-start.5
  136.0 57.3 %all-to-all-start.3 = ((bf16[8,176,1]{1,2,0:T(2,128)(2,1)}), bf16[8,176,1]{1,2,0:T(2,128)(2,1)S(1)}, u32[]{:S(2)}, u32[]{:S(2)}) async-start(bf16[8,176,1]{1,2,0:T(2,128)(2,1)} %convert_element_type.77), calls=%async_computation.3 | async-start | bytes 16384 | tf_op jit(solution)/shard_map/all_to_all | solution.py:76
  193.4 106.4 %all-to-all-start.2 = ((bf16[8,176,1152]{2,1,0:T(8,128)(2,1)}), bf16[8,176,1152]{2,1,0:T(8,128)(2,1)}, u32[]{:S(2)}, u32[]{:S(2)}) async-start(bf16[8,176,1152]{2,1,0:T(8,128)(2,1)} %bitcast.53), calls=%async_computation.2 | async-start | bytes 6488064 | tf_op jit(solution)/shard_map/all_to_all | solution.py:73
  198.0 88.2 %reduce-scatter.7.cloned.1.call-start = ((), (), s32[]{:S(2)}) async-start(), calls=%async_computation.9 | async-start | bytes 2985984
  208.7 135.0 %all-reduce.2.cloned.1.call-start = ((), (), s32[]{:S(2)}) async-start(), calls=%async_computation.8 | async-start | bytes 1179648 | tf_op jit(solution)/shard_map/psum | solution.py:93
Sparse Core Ops, SparseCore 0:
  38.9 38.9 all-gather.1
  135.4 55.9 reduce-scatter.4
  208.9 77.3 reduce-scatter.6
  289.7 53.9 all-reduce.1
where the time goes:
time: 353 us; the launch traced here: 352 us
  waiting for transfers between devices  219 us (62%)
  local copies, waits for them, and re-layouts  46.4 us (13%)
  matrix products  32.3 us (9%)
  starting transfers between devices  20.1 us (6%)
  other arithmetic  19.5 us (6%)
  between operations  15.2 us (4%)
    unnamed x5, waiting for transfers between devices  77.5 us
    all_to_all x1, waiting for transfers between devices, local(): lax.all_to_all(send_rows, 'group', split_axis=0, concat_axis=0, tiled=True)  68.4 us
    reduce_scatter x1, waiting for transfers between devices, local(): lax.psum_scatter(jnp.einsum('rc,rd->cd', pair_grad, x_half, preferred_ele...  39.5 us
    psum x1, waiting for transfers between devices, local(): head_grad = lax.psum(head_share, 'loop').astype(jnp.float32)  33.4 us
    unnamed x15, local copies, waits for them, and re-layouts  12 us
    dot_general x1, matrix products, local(): jnp.einsum('rd,cd->rc', x_half, captions, preferred_element_type=jnp.floa...  11.6 us
    gather x1, local copies, waits for them, and re-layouts, local(): view_loss = back_loss[slot_place]  11.3 us
    gather x1, local copies, waits for them, and re-layouts, local(): view_grad = back_rows[slot_place]  8.67 us
  transfers between devices with their start and end apart: 8, of which 4 were waited for; matrix products, arithmetic and copies ran while one was open for 19% of the time, Pallas kernels for 0%

commit v1 on v0

v1 whole, which is shorter than its diff:
```python
import functools

import jax
import jax.numpy as jnp
from jax import lax
from jax.experimental import pallas as pl
from jax.experimental.pallas import tpu as pltpu
from jax.sharding import PartitionSpec as P

epsilon = 1e-06
mates = 4
f32 = jnp.float32
bf16 = jnp.bfloat16
NN = (((1,), (0,)), ((), ()))
NT = (((1,), (1,)), ((), ()))


def dot(a, b, dims):
    return lax.dot_general(a, b, dims, preferred_element_type=f32)


def params(mib, **more):
    return pltpu.CompilerParams(vmem_limit_bytes=mib << 20, **more)


VMEM = pl.BlockSpec(memory_space=pltpu.VMEM)
SMEM = pl.BlockSpec(memory_space=pltpu.SMEM)


def log2_of(value):
    bits = value.bit_length() - 1
    assert 1 << bits == value
    return bits


def slot_ids(targets, rank, cluster, place, slots):
    mate = (targets & (mates - 1)) ^ place
    q = (targets >> 2) ^ cluster
    return (q * mates + mate) * slots + rank


def pack_kernel(cap, groups, slots, parts, members, where_ref, image_ref, views_ref, *refs):
    rows, width = views_ref.shape
    image = image_ref[...]
    if len(refs) > len(members):
        sid_ref, out_refs = refs[0], refs[1:]
        targets = (image >> log2_of(cap)) & (groups - 1)
        wide = max(groups, 16)
        chosen = (lax.broadcasted_iota(jnp.int32, (wide, rows), 0) == targets).astype(f32)
        before = (
            lax.broadcasted_iota(jnp.int32, (rows, rows), 0)
            < lax.broadcasted_iota(jnp.int32, (rows, rows), 1)
        ).astype(f32).astype(bf16)
        earlier = dot(chosen.astype(bf16), before, NN)
        rank = jnp.sum(earlier * chosen, axis=0, keepdims=True).astype(jnp.int32)
        sid = slot_ids(targets, rank, where_ref[0], where_ref[1], slots)
        sid_ref[...] = sid
    else:
        sid, out_refs = where_ref[...], refs
    local = (image & (cap - 1)).astype(f32)
    line = lax.broadcasted_iota(jnp.int32, (16, rows), 0)
    views = views_ref[...]
    slot = lax.broadcasted_iota(jnp.int32, (slots, rows), 0)
    for n, m in enumerate(members):
        hots = [(slot == sid - (q * mates + m) * slots).astype(f32).astype(bf16) for q in range(parts)]
        packed = dot(jnp.concatenate(hots, axis=0), views, NN)
        lines = jnp.zeros((16, slots), f32)
        for q, hot in enumerate(hots):
            info = jnp.where(line == q, local, jnp.where(line == parts + q, 1.0, 0.0)).astype(bf16)
            lines += dot(info, hot, NT)
        out_refs[n][: parts * slots, :] = packed.astype(bf16)
        out_refs[n][parts * slots :, :] = jnp.zeros((16, width), bf16)
        out_refs[n][parts * slots :, :slots] = lines.astype(bf16)


def caption_kernel(counts, weight_ref, *refs):
    feats, (half_ref, unit_ref, inverse_ref, turned_ref) = refs[:-4], refs[-4:]

    def block(pieces):
        value = jnp.concatenate([ref[...] for ref in pieces], axis=0)
        embed = dot(value, weight_ref[...], NN)
        inverse = lax.rsqrt(jnp.sum(embed * embed, axis=1, keepdims=True) + epsilon)
        unit = embed * inverse
        half_ref[...] = unit.astype(bf16)
        unit_ref[...] = unit
        inverse_ref[...] = jnp.broadcast_to(inverse, inverse_ref.shape)
        turned_ref[...] = value.T

    start = 0
    for k, count in enumerate(counts):
        pl.when(pl.program_id(0) == k)(functools.partial(block, feats[start : start + count]))
        start += count


def score_kernel(cap, q, parts, priors, scale_ref, offset_ref, a_ref, b_ref, ia_ref, ib_ref, count_ref, caps_ref, *refs):
    prior_refs, (va_ref, vb_ref, turned_ref, half_ref, loss_ref, pair_ref) = refs[:-6], refs[-6:]
    pair, slots = loss_ref.shape[:2]
    caps, width = caps_ref.shape
    scale, offset = scale_ref[0], offset_ref[0]
    eye = lax.broadcasted_iota(jnp.int32, (slots, slots), 0) == lax.broadcasted_iota(
        jnp.int32, (slots, slots), 1
    )
    held = [
        dot(eye.astype(f32).astype(bf16), ref[:, :slots], NT) for ref in (ia_ref, ib_ref)
    ]
    held = jnp.concatenate(held, axis=0)
    column = jnp.where(held[:, parts + q : parts + q + 1] > 0.5, held[:, q : q + 1], -1.0)
    named = lax.broadcasted_iota(jnp.int32, (pair * slots, cap), 1).astype(f32) == column
    weight = jnp.sum(
        jnp.where(named, 1.0 / count_ref[...].astype(f32), 0.0), axis=1, keepdims=True
    )
    factor = weight * scale
    x = jnp.concatenate([a_ref[...], b_ref[...]], axis=0).astype(f32)
    inverse = lax.rsqrt(jnp.sum(x * x, axis=1, keepdims=True) + epsilon)
    unit = x * inverse
    half = unit.astype(bf16)
    half_ref[: pair * slots, :] = half
    half_ref[pair * slots :, :] = jnp.zeros((half_ref.shape[0] - pair * slots, width), bf16)
    loss = jnp.zeros((pair * slots, 1), f32)
    for k in range(caps // cap):
        here = pl.ds(k * cap, cap)
        value = dot(half, caps_ref[here, :], NT) * scale + offset
        if k == 0:
            margin = jnp.where(named, -value, value)
        else:
            margin = value
        e = jnp.exp(-jnp.abs(margin))
        u = 1.0 + e
        r = 1.0 / u
        log1p = jnp.log(u) + (e - (u - 1.0)) * r
        loss = loss + jnp.sum(jnp.maximum(margin, 0.0) + log1p, axis=1, keepdims=True)
        grad = factor * jnp.where(margin >= 0.0, r, e * r)
        if k == 0:
            grad = jnp.where(named, -grad, grad)
        pair_ref[:, here] = grad.astype(bf16)
        turned_ref[here, : pair * slots] = grad.T.astype(bf16)
        turned_ref[here, pair * slots :] = jnp.zeros((cap, turned_ref.shape[1] - pair * slots), bf16)
    grad_x = dot(pair_ref[...], caps_ref[...], NN)
    grad_v = (grad_x - unit * jnp.sum(unit * grad_x, axis=1, keepdims=True)) * inverse
    grad_v = grad_v.astype(bf16)
    loss = loss * (1.0 / caps)
    for m, back_ref in enumerate((va_ref, vb_ref)):
        back_ref[:slots, :] = grad_v[m * slots : (m + 1) * slots]
    for m in range(pair):
        loss_ref[m] = jnp.broadcast_to(loss[m * slots : (m + 1) * slots], (slots, 128))
    if va_ref.shape[0] > slots:
        ones = jnp.ones((16, slots), bf16)
        line = lax.broadcasted_iota(jnp.int32, (16, slots), 0)
        for m, back_ref in enumerate((va_ref, vb_ref)):
            columns = [(p, ref[m][:, 0:1]) for p, ref in zip(priors, prior_refs)]
            columns.append((q, loss[m * slots : (m + 1) * slots]))
            lines = jnp.zeros((16, slots), f32)
            for p, value in columns:
                lines += jnp.where(line == p, dot(ones, jnp.where(eye, value, 0.0).astype(bf16), NN), 0.0)
            back_ref[slots:, :] = jnp.zeros((16, width), bf16)
            back_ref[slots:, :slots] = lines.astype(bf16)


def caption_grad_kernel(pa_ref, pb_ref, xa_ref, xb_ref, unit_ref, inverse_ref, out_ref):
    pairs = jnp.concatenate([pa_ref[...], pb_ref[...]], axis=1)
    total = dot(pairs, jnp.concatenate([xa_ref[...], xb_ref[...]], axis=0), NN)
    unit = unit_ref[...]
    total = total - unit * jnp.sum(unit * total, axis=1, keepdims=True)
    out_ref[...] = (total * inverse_ref[:, 0:1]).astype(bf16)


def unpack_kernel(slots, parts, part, sid_ref, *refs):
    backs, refs = refs[:mates], refs[mates:]
    rows = sid_ref.shape[1]
    last = len(refs) > 1
    many = mates * slots
    sid = jnp.broadcast_to(sid_ref[...].astype(f32), (128, rows)).T[:, 0:1].astype(jnp.int32)
    lanes = lax.broadcasted_iota(jnp.int32, (rows, many), 1)

    def hot(q):
        return (lanes == sid - q * many).astype(f32).astype(bf16)

    back = jnp.concatenate([ref[:slots, :] for ref in backs], axis=0)
    result = dot(hot(part), back, NN)
    if last:
        lines, (before_ref, out_ref, loss_ref) = refs[:mates], refs[mates:]
        result = result + before_ref[...].astype(f32)
    else:
        (out_ref,) = refs
    out_ref[...] = result.astype(bf16)
    if last:
        losses = jnp.zeros((16, rows), f32)
        for q in range(parts):
            line = jnp.concatenate([ref[:, :slots] for ref in lines], axis=1)
            mine = lax.broadcasted_iota(jnp.int32, line.shape, 0) == q
            line = jnp.where(mine, line.astype(f32), 0.0).astype(bf16)
            losses += dot(line, hot(q), NT)
        loss_ref[...] = jnp.sum(losses, axis=0, keepdims=True)


def after(value, *others):
    return lax.optimization_barrier((value, *others))[0]


def with_order(kernel, count):
    return lambda *refs: kernel(*refs[count:])


ANY = pl.BlockSpec(memory_space=pl.ANY)


def cost(flops, read, wrote):
    return pl.CostEstimate(flops=flops, bytes_accessed=read + wrote, transcendentals=0)


def local(view_embeds, view_image, view_counts, text_feats, head_weight, logit_scale, logit_bias):
    cap = view_counts.shape[0]
    rows, width = view_embeds.shape
    groups = lax.axis_size("group")
    loops = lax.axis_size("loop")
    parts = groups // mates
    slots = -(-(11 * cap // (2 * groups)) // 16) * 16
    pair_slots = -(-2 * slots // 128) * 128
    caps = cap * loops
    me = lax.axis_index("group")
    lane = lax.axis_index("loop")
    cluster, place = me // mates, me % mates

    def over(axis, size, value, mask):
        return lax.ppermute(value, axis, [(i, i ^ mask) for i in range(size)])

    def over_loop(value, mask):
        return over("loop", loops, value, mask)

    def over_group(value, mask):
        return over("group", groups, value, mask)

    def bits_of(k):
        return [1 << b for b in range(k.bit_length()) if k >> b & 1][:2]

    in_order = sorted(range(1, loops), key=lambda k: (bin(k).count("1"), k))

    def gather_loop(block):
        pieces = {0: [block]}
        for k in in_order:
            bits = bits_of(k)
            if len(bits) == 1:
                pieces[k] = [over_loop(block, k)]
                continue
            pieces[k] = []
            for i, bit in enumerate(bits):
                source = pieces[k ^ bit]
                half = source[i] if len(source) == 2 else lax.slice_in_dim(source[0], i * cap // 2, (i + 1) * cap // 2)
                pieces[k].append(over_loop(half, bit))
        return pieces

    def scatter_loop(terms):
        half = cap // 2
        total = {(k, i): terms[k, i * half : (i + 1) * half] for k in range(loops) for i in range(2)}
        bit = {(k, i): bits_of(k)[i % len(bits_of(k))] for k, i in total if k}
        children = {at: [way for way in bit if way[1] == at[1] and way[0] ^ bit[way] == at[0]] for at in total}

        def depth(at):
            return 1 + max((depth(child) for child in children[at]), default=-1)

        waves = {}
        for at in bit:
            waves.setdefault((depth(at), bit[at]), []).append(at)
        marks = []
        for (_, way), members in sorted(waves.items()):
            sent = [total[at].astype(bf16) for at in members]
            got = over_loop(jnp.concatenate(sent) if len(sent) > 1 else sent[0], way)
            marks.append(got)
            for n, (k, i) in enumerate(members):
                parent = (k ^ way, i)
                total[parent] = total[parent].astype(f32) + got[n * half : (n + 1) * half].astype(f32)
        return jnp.concatenate([total[0, 0], total[0, 1]], axis=0), marks

    where = jnp.stack([cluster, place]).astype(jnp.int32)

    feats = [text_feats] + [over_group(text_feats, mates * q) for q in range(1, parts)]
    counts = [view_counts] + [over_group(view_counts, mates * q) for q in range(1, parts)]
    counts = [value.reshape(1, cap) for value in counts]

    row = jax.ShapeDtypeStruct((parts * slots + 16, width), bf16)
    def pack(members, where, *more):
        many = parts * len(members) * slots
        return pl.pallas_call(
            functools.partial(pack_kernel, cap, groups, slots, parts, members),
            out_shape=list(more) + [row] * len(members),
            in_specs=[SMEM if more else VMEM, VMEM, VMEM],
            out_specs=[VMEM] * (len(more) + len(members)),
            compiler_params=params(56),
            cost_estimate=cost(2 * many * rows * width, rows * width * 2, many * width * 2),
            name="pack",
        )(where, view_image.reshape(1, rows), view_embeds)

    sid, *far_rows = pack((2, 3), where, jax.ShapeDtypeStruct((1, rows), jnp.int32))
    packed = [*pack((0, 1), sid), *far_rows]
    moved = {m: over_group(packed[m], m) for m in (2, 3, 1)}
    held = [packed[0]] + [moved[m] for m in range(1, mates)]

    def caption(q, gathered, *before):
        pieces = [piece for k in range(loops) for piece in gathered[k]]
        return (
            pl.pallas_call(
                with_order(
                    functools.partial(caption_kernel, [len(gathered[k]) for k in range(loops)]), len(before)
                ),
                grid=(loops,),
                out_shape=[
                    jax.ShapeDtypeStruct((caps, width), bf16),
                    jax.ShapeDtypeStruct((caps, width), f32),
                    jax.ShapeDtypeStruct((caps, 128), f32),
                    jax.ShapeDtypeStruct((width, caps), bf16),
                ],
                in_specs=[ANY] * len(before)
                + [pl.BlockSpec(value.shape, lambda k: (0, 0)) for value in [head_weight, *pieces]],
                out_specs=[pl.BlockSpec((cap, wide), lambda k: (k, 0)) for wide in (width, width, 128)]
                + [pl.BlockSpec((width, cap), lambda k: (0, k))],
                compiler_params=params(56),
                cost_estimate=cost(2 * caps * width * width, (caps + width) * width * 2, caps * width * 8),
                name="captions",
            )(*before, head_weight, *pieces)
        )

    def score(q, first, losses, *before):
        carry = len(losses) == parts - 1
        priors = list(losses) if carry else []
        sent = jax.ShapeDtypeStruct((slots + (16 if carry else 0), width), bf16)
        return pl.pallas_call(
            with_order(functools.partial(score_kernel, cap, q, parts, priors), len(before)),
            grid=(1,),
            out_shape=[
                sent,
                sent,
                jax.ShapeDtypeStruct((caps, pair_slots), bf16),
                jax.ShapeDtypeStruct((pair_slots, width), bf16),
                jax.ShapeDtypeStruct((2, slots, 128), f32),
            ],
            in_specs=[ANY] * len(before)
            + [
                SMEM,
                SMEM,
                pl.BlockSpec((slots, width), lambda i: (q, 0)),
                pl.BlockSpec((slots, width), lambda i: (q, 0)),
                pl.BlockSpec((16, width), lambda i: (parts * slots // 16, 0)),
                pl.BlockSpec((16, width), lambda i: (parts * slots // 16, 0)),
                pl.BlockSpec((1, cap), lambda i: (0, 0)),
                pl.BlockSpec((caps, width), lambda i: (0, 0)),
            ]
            + [pl.BlockSpec((2, slots, 128), lambda i: (0, 0, 0))] * len(priors),
            scratch_shapes=[pltpu.VMEM((2 * slots, caps), bf16)],
            compiler_params=params(56),
            cost_estimate=cost(8 * slots * caps * width, (2 * slots + caps) * width * 2, slots * width * 12),
            name="score",
        )(
            *before, logit_scale, logit_bias, *[held[first + i % 2] for i in range(4)], counts[q], captions[q][0],
            *[losses[p] for p in priors],
        )

    def caption_grad(q, near, far, *before):
        return pl.pallas_call(
            with_order(caption_grad_kernel, len(before)),
            grid=(loops,),
            out_shape=jax.ShapeDtypeStruct((caps, width), bf16),
            in_specs=[ANY] * len(before)
            + [
                pl.BlockSpec((cap, pair_slots), lambda k: (k, 0)),
                pl.BlockSpec((cap, pair_slots), lambda k: (k, 0)),
                pl.BlockSpec((pair_slots, width), lambda k: (0, 0)),
                pl.BlockSpec((pair_slots, width), lambda k: (0, 0)),
                pl.BlockSpec((cap, width), lambda k: (k, 0)),
                pl.BlockSpec((cap, 128), lambda k: (k, 0)),
            ],
            out_specs=pl.BlockSpec((cap, width), lambda k: (k, 0)),
            compiler_params=params(56),
            cost_estimate=cost(
                2 * mates * slots * caps * width, caps * width * 4 + mates * slots * width * 4, caps * width * 2
            ),
            name="caption_grad",
        )(*before, near[2], far[2], near[3], far[3], captions[q][1], captions[q][2])

    def unpack(q, result, *before):
        last = result is not None
        whole = pl.BlockSpec((rows, width), lambda i: (0, 0))
        line = pl.BlockSpec((1, rows), lambda i: (0, 0))
        return pl.pallas_call(
            with_order(functools.partial(unpack_kernel, slots, parts, q), len(before)),
            grid=(1,),
            out_shape=[jax.ShapeDtypeStruct((rows, width), bf16)]
            + [jax.ShapeDtypeStruct((1, rows), f32)] * last,
            in_specs=[ANY] * len(before)
            + [line]
            + [pl.BlockSpec((slots, width), lambda i: (0, 0))] * mates
            + [pl.BlockSpec((16, width), lambda i: (slots // 16, 0))] * (mates * last)
            + [whole] * last,
            out_specs=[whole] + [line] * last,
            compiler_params=params(56),
            cost_estimate=cost(2 * mates * slots * rows * width, mates * slots * width * 2, rows * width * 2),
            name="unpack",
        )(*before, sid, *back[q], *(carriers + [result] if last else []))

    captions, near, far, grads, back, sums, marks = {}, {}, {}, {}, {}, {}, {}
    there = {q: {} for q in range(parts)}
    token = packed[:1]
    for q in range(parts):
        gathered = gather_loop(after(feats[q], token[0]) if q else feats[q])
        captions[q] = caption(q, gathered, *token)
        token = [captions[q][2]]
        if q < parts - 1:
            near[q] = score(q, 0, {p: near[p][4] for p in near}, *token)
            there[q][1] = over_group(near[q][1], 1)
            token = [near[q][4], there[q][1]]
            if q:
                token = token[:1]
    for q in reversed(range(parts)):
        far[q] = score(q, 2, {p: far[p][4] for p in far}, *token)
        there[q][2], there[q][3] = over_group(far[q][0], 2), over_group(far[q][1], 3)
        token = []
        if q == parts - 1:
            near[q] = score(q, 0, {p: near[p][4] for p in near}, far[q][4])
            there[q][1] = over_group(near[q][1], 1)
            token = [there[q][1]]
        back[q] = [near[q][0], there[q][1], there[q][2], there[q][3]]
        grads[q] = caption_grad(q, near[q], far[q])
        token.append(grads[q])
        sums[q], marks[q] = scatter_loop(grads[q].reshape(loops, cap, width))
    carriers = back[parts - 1][:2] + back[0][2:]

    total = sums[0]
    for q in range(1, parts):
        total = total + over_group(sums[q].astype(bf16), mates * q).astype(f32)
    text_grad = jnp.einsum(
        "cd,ed->ce", total.astype(bf16), head_weight, preferred_element_type=f32
    ).astype(bf16)

    share = width // groups
    head = sum(
        dot(captions[q][3], after(grads[q], *marks[parts - 1][:2]), NN) for q in range(parts)
    )
    head = head.astype(bf16)
    head = after(head, *marks[parts - 1][2:], *back[parts - 1][2:])
    head = head.reshape(groups // 2, 2, share, width)
    core = me % 2
    got = over_group(lax.dynamic_index_in_dim(head, 1 - core, 1, keepdims=False), 1)
    head = lax.dynamic_index_in_dim(head, core, 1, keepdims=False).astype(f32) + got.astype(f32)
    head = head.astype(bf16).reshape(groups // 2, loops, share // loops, width)
    piece = lax.dynamic_index_in_dim(head, lane, 1, keepdims=False).astype(f32)
    for k in range(1, loops):
        piece += over_loop(lax.dynamic_index_in_dim(head, lane ^ k, 1, keepdims=False), k).astype(f32)
    head = piece.astype(bf16)
    height = me // 2
    piece = lax.dynamic_index_in_dim(head, height, 0, keepdims=False).astype(f32)
    for k in range(1, groups // 2):
        piece += over_group(lax.dynamic_index_in_dim(head, height ^ k, 0, keepdims=False), 2 * k).astype(f32)
    piece = piece.astype(bf16)
    whole = jnp.stack([piece] + [over_loop(piece, k) for k in range(1, loops)])
    whole = whole[lane ^ jnp.arange(loops, dtype=jnp.int32)]
    head_grad = whole.reshape(share, width).astype(f32)

    result = None
    for q in reversed(range(parts)):
        result = unpack(q, result[0] if result else None)
    view_grad, view_loss = result
    view_loss = view_loss.reshape(rows).astype(bf16)
    return (view_grad, view_loss, text_grad, head_grad)


def solution(mesh):
    return jax.shard_map(
        local,
        mesh=mesh,
        in_specs=(
            P(("loop", "group"), None),
            P(("loop", "group")),
            P(("loop", "group")),
            P(("loop", "group"), None),
            P(),
            P(),
            P(),
        ),
        out_specs=(
            P(("loop", "group"), None),
            P(("loop", "group")),
            P(("loop", "group"), None),
            P("group", None),
        ),
        check_vma=False,
    )
```

time: 353 us -> 220 us (0.62)
  waiting for transfers between devices: 219 us -> 58.9 us
  Pallas kernels: 0 us -> 81.3 us
  local copies, waits for them, and re-layouts: 46.4 us -> 9.12 us
  starting transfers between devices: 20.1 us -> 44.3 us
  matrix products: 32.3 us -> 10.7 us
  between operations: 15.2 us -> 2.53 us
  other arithmetic: 19.5 us -> 9.16 us
    pallas_call x0 -> x12, Pallas kernels: none -> 81.3 us  [the longest x4 24.8 us: score(): pl.pallas_call(with_order(functools.partial(score_kernel, cap, q, parts,...]
    unnamed x5 -> x0, waiting for transfers between devices: 77.5 us -> none
    all_to_all x4 -> x0, waiting for transfers between devices: 68.4 us -> none  [the longest x1 68.4 us: local(): lax.all_to_all(send_rows, 'group', split_axis=0, concat_axis=0, tiled=True)]
    ppermute x0 -> x38, waiting for transfers between devices: none -> 58.9 us  [over(): return lax.ppermute(value, axis, [(i, i ^ mask) for i in range(size)])]
    ppermute x0 -> x38, starting transfers between devices: none -> 44.3 us  [over(): return lax.ppermute(value, axis, [(i, i ^ mask) for i in range(size)])]
    reduce_scatter x1 -> x0, waiting for transfers between devices: 39.5 us -> none  [local(): lax.psum_scatter(jnp.einsum('rc,rd->cd', pair_grad, x_half, preferred_ele...]
    psum x1 -> x0, waiting for transfers between devices: 33.4 us -> none  [local(): head_grad = lax.psum(head_share, 'loop').astype(jnp.float32)]
    dot_general x6 -> x3, matrix products: 32.3 us -> 10.7 us  [the longest x2 8.79 us: dot(): return lax.dot_general(a, b, dims, preferred_element_type=f32)]
  transfers between devices with their start and end apart: 8 -> 38, of which waited for: 4 -> 16; matrix products, arithmetic and copies ran while one was open for 19% -> 10% of each run, Pallas kernels for 0% -> 28%
where the time goes in v1:
time: 220 us; the launch traced here: 216 us
  Pallas kernels  81.3 us (37%)
  waiting for transfers between devices  58.9 us (27%)
  starting transfers between devices  44.3 us (20%)
  matrix products  10.7 us (5%)
  other arithmetic  9.16 us (4%)
  local copies, waits for them, and re-layouts  9.12 us (4%)
  between operations  2.53 us (1%)
    ppermute x38, waiting for transfers between devices, over(): return lax.ppermute(value, axis, [(i, i ^ mask) for i in range(size)])  58.9 us
    ppermute x38, starting transfers between devices, over(): return lax.ppermute(value, axis, [(i, i ^ mask) for i in range(size)])  44.3 us
    pallas_call x4, Pallas kernels, score(): pl.pallas_call(with_order(functools.partial(score_kernel, cap, q, parts,...  24.8 us
    pallas_call x2, Pallas kernels, caption(): pl.pallas_call(with_order(functools.partial(caption_kernel, [len(gathered...  18.6 us
    pallas_call x2, Pallas kernels, caption_grad(): pl.pallas_call(with_order(caption_grad_kernel, len(before)), grid=(loops,...  14.9 us
    pallas_call x2, Pallas kernels, unpack(): pl.pallas_call(with_order(functools.partial(unpack_kernel, slots, parts,...  12.6 us
    pallas_call x2, Pallas kernels, pack(): pl.pallas_call(functools.partial(pack_kernel, cap, groups, slots, parts,...  10.4 us
    dot_general x2, matrix products, dot(): return lax.dot_general(a, b, dims, preferred_element_type=f32)  8.79 us
  transfers between devices with their start and end apart: 38, of which 16 were waited for; matrix products, arithmetic and copies ran while one was open for 10% of the time, Pallas kernels for 28%

profile of v1, /device:TPU:0, one launch (start us, length us, event | category | flops | bytes accessed | tf_op | source)
XLA Modules:
  0.0 215.9 jit_solution(7762857189359360544)
XLA Ops:
  0.6 3.0 %collective-permute-start.1 = (bf16[256,1152]{1,0:T(8,128)(2,1)}, bf16[256,1152]{1,0:T(8,128)(2,1)S(1)}, u32[]{:S(2)}, u32[]{:S(2)}) collective-permute-start(bf16[256,1152]{1,0:T(8,128)(2,1)} %refs_2_.6), channel_id=1, source_target_pairs={{0,16},{8,24},{16,0},{24,8},{1,17},{9,25},{17,1},{25,9},{2,18},{10... | collective-permute-start | bytes 1769480 | tf_op jit(solution)/shard_map/ppermute | solution.py:225
  3.7 1.5 collective-permute-start
  5.7 5.3 %pack.2 = (s32[1,1024]{1,0:T(1,128)}, bf16[368,1152]{1,0:T(8,128)(2,1)}, bf16[368,1152]{1,0:T(8,128)(2,1)}) custom-call(s32[2]{0:T(128)} %pad_add_fusion.where_ref, s32[1,1024]{1,0:T(1,128)} %bitcast.133, bf16[1024,1152]{1,0:T(8,128)(2,1)} %views_ref.3), custom_call_target="tpu_custom_call" | custom-call | flops 1660944384 | bytes 3981312 | tf_op jit(solution)/shard_map/pack/pallas_call | solution.py:283
  11.1 5.1 %pack.3 = (bf16[368,1152]{1,0:T(8,128)(2,1)}, bf16[368,1152]{1,0:T(8,128)(2,1)}) custom-call(s32[1,1024]{1,0:T(1,128)} %get-tuple-element.41.where_ref.refs_0_, s32[1,1024]{1,0:T(1,128)} %bitcast.134, bf16[1024,1152]{1,0:T(8,128)(2,1)} %views_ref.3), custom_call_target="tpu_custom_call" | custom-call | flops 1660944384 | bytes 3981312 | tf_op jit(solution)/shard_map/pack/pallas_call | solution.py:283
  16.1 1.1 collective-permute-done.1.refs_4_
  17.2 1.8 collective-permute-start.2
  19.0 1.6 collective-permute-start.3
  20.6 2.6 %collective-permute-start.6 = (bf16[256,1152]{1,0:T(8,128)(2,1)S(1)}, bf16[256,1152]{1,0:T(8,128)(2,1)S(1)}, u32[]{:S(2)}, u32[]{:S(2)}) collective-permute-start(bf16[256,1152]{1,0:T(8,128)(2,1)S(1)} %copy-done.16), channel_id=1, source_target_pairs={{0,4},{1,5},{2,6},{3,7},{4,0},{5,1},{6,2},{7,3},{8,12},{9,13},{10,... | collective-permute-start | bytes 1769480 | tf_op jit(solution)/shard_map/ppermute | solution.py:225
  24.5 1.1 collective-permute-done.2.refs_5_
  25.7 1.0 collective-permute-done.3.refs_6_
  27.4 9.4 %captions.2 = (bf16[1024,1152]{1,0:T(8,128)(2,1)}, f32[1024,1152]{1,0:T(8,128)}, f32[1024,128]{1,0:T(8,128)}, bf16[1152,1024]{1,0:T(8,128)(2,1)}) custom-call(bf16[368,1152]{1,0:T(8,128)(2,1)} %get-tuple-element.42.refs_0_.refs_3_.refs_5_, bf16[1152,1152]{1,0:T(8,128)(2,1)} %refs_2_.7, bf16[256,1152]{1,0:T(8,128)(2,1)} %refs_2_.6, ...), custom_call_target="tpu_custom_call" | custom-call | flops 2717908992 | bytes 14450688 | tf_op jit(solution)/shard_map/captions/pallas_call | solution.py:301
  36.9 0.9 copy-done.4
  37.8 6.2 %score.4 = (bf16[176,1152]{1,0:T(8,128)(2,1)}, bf16[176,1152]{1,0:T(8,128)(2,1)}, bf16[1024,384]{1,0:T(8,128)(2,1)}, bf16[384,1152]{1,0:T(8,128)(2,1)}, f32[2,176,128]{2,1,0:T(8,128)}) custom-call(f32[1024,128]{1,0:T(8,128)} %get-tuple-element.43.refs_0_.refs_5_, f32[1]{0:T(128)S(6)} %copy.32.refs_1_.refs_2_, f32[1]{0:T(128)S(6)} %copy.33.refs_2_.refs_3_, ...), custom_call_target="tpu_custom_call" | custom-call | flops 1660944384 | bytes 5603328 | tf_op jit(solution)/shard_map/score/pallas_call | solution.py:326
  44.0 3.8 %collective-permute-done.6.refs_3_ = bf16[256,1152]{1,0:T(8,128)(2,1)S(1)} collective-permute-done((bf16[256,1152]{1,0:T(8,128)(2,1)S(1)}, bf16[256,1152]{1,0:T(8,128)(2,1)S(1)}, u32[]{:S(2)}, u32[]{:S(2)}) %collective-permute-start.6) | collective-permute-done | bytes 589856 | tf_op jit(solution)/shard_map/ppermute | solution.py:225
  48.3 1.1 collective-permute-start.8
  50.1 1.5 collective-permute-start.5
  51.6 10.4 %collective-permute-done.7.refs_4_ = bf16[256,1152]{1,0:T(8,128)(2,1)S(1)} collective-permute-done((bf16[256,1152]{1,0:T(8,128)(2,1)S(1)}, bf16[256,1152]{1,0:T(8,128)(2,1)S(1)}, u32[]{:S(2)}, u32[]{:S(2)}) %collective-permute-start.7) | collective-permute-done | bytes 589856 | tf_op jit(solution)/shard_map/ppermute | solution.py:225
  62.6 1.6 collective-permute-start.9
  64.4 4.7 %collective-permute-done.10.refs_7_ = bf16[128,1152]{1,0:T(8,128)(2,1)} collective-permute-done((bf16[128,1152]{1,0:T(8,128)(2,1)S(1)}, bf16[128,1152]{1,0:T(8,128)(2,1)}, u32[]{:S(2)}, u32[]{:S(2)}) %collective-permute-start.10) | collective-permute-done | bytes 294944 | tf_op jit(solution)/shard_map/ppermute | solution.py:225
  69.5 9.1 %captions.3 = (bf16[1024,1152]{1,0:T(8,128)(2,1)}, f32[1024,1152]{1,0:T(8,128)}, f32[1024,128]{1,0:T(8,128)}, bf16[1152,1024]{1,0:T(8,128)(2,1)}) custom-call(f32[2,176,128]{2,1,0:T(8,128)} %get-tuple-element.48.refs_0_.refs_9_, bf16[176,1152]{1,0:T(8,128)(2,1)} %collective-permute-done.5.refs_1_.refs_2_, bf16[1152,1152]{1,0:T(8,128)(2,1)} %refs_2_.7, ...), custom_call_target="tpu_custom_call" | custom-call | flops 2717908992 | bytes 14450688 | tf_op jit(solution)/shard_map/captions/pallas_call | solution.py:301
  78.6 7.7 %collective-permute-done.13 = s32[256]{0:T(256)S(1)} collective-permute-done((s32[256]{0:T(256)S(1)}, s32[256]{0:T(256)S(1)}, u32[]{:S(2)}, u32[]{:S(2)}) %collective-permute-start.13) | collective-permute-done | bytes 1056 | tf_op jit(solution)/shard_map/ppermute | solution.py:225
  87.5 6.2 %score.5 = (bf16[176,1152]{1,0:T(8,128)(2,1)}, bf16[176,1152]{1,0:T(8,128)(2,1)}, bf16[1024,384]{1,0:T(8,128)(2,1)}, bf16[384,1152]{1,0:T(8,128)(2,1)}, f32[2,176,128]{2,1,0:T(8,128)}) custom-call(f32[1024,128]{1,0:T(8,128)} %get-tuple-element.50.refs_0_.refs_5_, f32[1]{0:T(128)S(6)} %copy.32.refs_1_.refs_2_, f32[1]{0:T(128)S(6)} %copy.33.refs_2_.refs_3_, ...), custom_call_target="tpu_custom_call" | custom-call | flops 1660944384 | bytes 5603328 | tf_op jit(solution)/shard_map/score/pallas_call | solution.py:326
  93.8 6.2 %score.6 = (bf16[192,1152]{1,0:T(8,128)(2,1)}, bf16[192,1152]{1,0:T(8,128)(2,1)}, bf16[1024,384]{1,0:T(8,128)(2,1)}, bf16[384,1152]{1,0:T(8,128)(2,1)}, f32[2,176,128]{2,1,0:T(8,128)}) custom-call(f32[2,176,128]{2,1,0:T(8,128)} %get-tuple-element.54.refs_0_.refs_10_, f32[1]{0:T(128)S(6)} %copy.32.refs_1_.refs_2_, f32[1]{0:T(128)S(6)} %copy.33.refs_2_.refs_3_, ...), custom_call_target="tpu_custom_call" | custom-call | flops 1660944384 | bytes 5603328 | tf_op jit(solution)/shard_map/score/pallas_call | solution.py:326
  100.0 7.3 %caption_grad.2.refs_1_ = bf16[1024,1152]{1,0:T(8,128)(2,1)} custom-call(bf16[1024,384]{1,0:T(8,128)(2,1)} %get-tuple-element.56.refs_0_, bf16[1024,384]{1,0:T(8,128)(2,1)} %get-tuple-element.57.refs_1_, bf16[384,1152]{1,0:T(8,128)(2,1)} %get-tuple-element.58.refs_2_, bf16[384,1152]{1,0:T(8,128)(2,1)} %get-tuple-element.59.refs_3_, ...), custom_call_target="tpu_custom_call" | custom-call | flops 1660944384 | bytes 10321920 | tf_op jit(solution)/shard_map/caption_grad/pallas_call | solution.py:358
  107.4 1.4 slice_bitcast_fusion.6
  109.1 1.0 collective-permute-start.25
  110.1 1.6 collective-permute-start.23
  111.7 3.9 %collective-permute-start.17 = (bf16[176,1152]{1,0:T(8,128)(2,1)S(1)}, bf16[176,1152]{1,0:T(8,128)(2,1)S(1)}, u32[]{:S(2)}, u32[]{:S(2)}) collective-permute-start(bf16[176,1152]{1,0:T(8,128)(2,1)S(1)} %copy-done.20), channel_id=1, source_target_pairs={{0,2},{1,3},{2,0},{3,1},{4,6},{5,7},{6,4},{7,5},{8,10},{9,11},{10,... | collective-permute-start | bytes 1216520 | tf_op jit(solution)/shard_map/ppermute | solution.py:225
  116.3 6.1 %score.7 = (bf16[192,1152]{1,0:T(8,128)(2,1)}, bf16[192,1152]{1,0:T(8,128)(2,1)}, bf16[1024,384]{1,0:T(8,128)(2,1)}, bf16[384,1152]{1,0:T(8,128)(2,1)}, f32[2,176,128]{2,1,0:T(8,128)}) custom-call(bf16[192,1152]{1,0:T(8,128)(2,1)} %copy-done.7, bf16[1024,1152]{1,0:T(8,128)(2,1)} %caption_grad.2.refs_1_, f32[1]{0:T(128)S(6)} %copy.32.refs_1_.refs_2_, ...), custom_call_target="tpu_custom_call" | custom-call | flops 1660944384 | bytes 5603328 | tf_op jit(solution)/shard_map/score/pallas_call | solution.py:326
  122.5 7.5 %caption_grad.3 = bf16[1024,1152]{1,0:T(8,128)(2,1)} custom-call(bf16[1024,384]{1,0:T(8,128)(2,1)} %get-tuple-element.68.refs_0_, bf16[1024,384]{1,0:T(8,128)(2,1)} %get-tuple-element.69.refs_1_, bf16[384,1152]{1,0:T(8,128)(2,1)} %get-tuple-element.70.refs_2_, bf16[384,1152]{1,0:T(8,128)(2,1)} %get-tuple-element.71.refs_3_, ...), custom_call_target="tpu_custom_call" | custom-call | flops 1660944384 | bytes 10321920 | tf_op jit(solution)/shard_map/caption_grad/pallas_call | solution.py:358
  130.0 1.3 slice_bitcast_fusion.14
  131.3 0.9 pad_maximum_fusion.1
  133.6 1.1 collective-permute-start.19
  134.7 1.3 collective-permute-start.15
  135.9 5.5 %unpack.2.refs_9_ = bf16[1024,1152]{1,0:T(8,128)(2,1)} custom-call(s32[1,1024]{1,0:T(1,128)} %get-tuple-element.41.where_ref.refs_0_, bf16[192,1152]{1,0:T(8,128)(2,1)} %get-tuple-element.63.refs_1_.refs_5_, bf16[192,1152]{1,0:T(8,128)(2,1)} %copy-done.7, bf16[176,1152]{1,0:T(8,128)(2,1)} %copy-done.21, bf16[176,1152]{1,0:T(8,128)(2,1)} %copy-done.22), custom_call_target="tpu_custom_call" | custom-call | flops 1660944384 | bytes 3981312 | tf_op jit(solution)/shard_map/unpack/pallas_call | solution.py:383
  142.2 1.0 collective-permute-start.24
  143.2 5.0 %fusion.22 = f32[1152,1152]{1,0:T(8,128)S(1)} fusion(bf16[1152,1024]{1,0:T(8,128)(2,1)} %get-tuple-element.75, bf16[1024,1152]{1,0:T(8,128)(2,1)S(1)} %copy-done), kind=kOutput, calls=%fused_computation.76 | convolution fusion | flops 2717908992 | bytes 10027008 | tf_op jit(solution)/shard_map/dot_general | solution.py:19
  148.3 5.8 %collective-permute-done.24 = bf16[128,1152]{1,0:T(8,128)(2,1)S(1)} collective-permute-done((bf16[128,1152]{1,0:T(8,128)(2,1)S(1)}, bf16[128,1152]{1,0:T(8,128)(2,1)S(1)}, u32[]{:S(2)}, u32[]{:S(2)}) %collective-permute-start.24) | collective-permute-done | bytes 294944 | tf_op jit(solution)/shard_map/ppermute | solution.py:225
  154.1 0.9 fusion.12
  155.6 3.7 %fusion = bf16[1152,1152]{1,0:T(8,128)(2,1)S(1)} fusion(f32[1152,1152]{1,0:T(8,128)S(1)} %fusion.22, bf16[1152,1024]{1,0:T(8,128)(2,1)S(1)} %copy-done.25, bf16[1024,1152]{1,0:T(8,128)(2,1)S(1)} %copy-done.3), kind=kOutput, calls=%fused_computation.2 | convolution fusion | flops 2720563200 | bytes 12681216 | tf_op jit(solution)/shard_map/dot_general | solution.py:19
  159.4 7.1 %unpack.3 = (bf16[1024,1152]{1,0:T(8,128)(2,1)}, f32[1,1024]{1,0:T(1,128)}) custom-call(s32[1,1024]{1,0:T(1,128)} %get-tuple-element.41.where_ref.refs_0_, bf16[176,1152]{1,0:T(8,128)(2,1)} %get-tuple-element.46.refs_1_, bf16[176,1152]{1,0:T(8,128)(2,1)} %collective-permute-done.5.refs_1_.refs_2_, bf16[192,1152]{1,0:T(8,128)(2,1)} %collective-permute-done.15.refs_3_.refs_7_, ...), custom_call_target="tpu_custom_call" | custom-call | flops 1660944384 | bytes 3981312 | tf_op jit(solution)/shard_map/unpack/pallas_call | solution.py:383
  168.0 1.1 collective-permute-start.20
  169.2 1.1 fusion.9
  170.3 1.5 collective-permute-start.27
  172.8 1.0 collective-permute-start.29
  173.8 1.5 collective-permute-start.30
  175.3 1.1 collective-permute-start.31
  176.4 1.5 collective-permute-done.20
  177.9 1.1 fusion.16
  179.0 1.6 collective-permute-start.22
  180.6 3.0 %collective-permute-done.29 = bf16[4,36,1152]{2,0,1:T(4,128)(2,1)S(1)} collective-permute-done((bf16[4,36,1152]{2,0,1:T(4,128)(2,1)S(1)}, bf16[4,36,1152]{2,0,1:T(4,128)(2,1)S(1)}, u32[]{:S(2)}, u32[]{:S(2)}) %collective-permute-start.29) | collective-permute-done | bytes 331808 | tf_op jit(solution)/shard_map/ppermute | solution.py:225
  183.6 8.1 %collective-permute-done.30 = bf16[4,36,1152]{2,0,1:T(4,128)(2,1)S(1)} collective-permute-done((bf16[4,36,1152]{2,0,1:T(4,128)(2,1)S(1)}, bf16[4,36,1152]{2,0,1:T(4,128)(2,1)S(1)}, u32[]{:S(2)}, u32[]{:S(2)}) %collective-permute-start.30) | collective-permute-done | bytes 331808 | tf_op jit(solution)/shard_map/ppermute | solution.py:225
  192.7 2.0 collective-permute-start.32
  194.7 1.0 collective-permute-start.33
  195.7 1.6 collective-permute-start.34
  197.3 1.1 fusion.14
  198.4 2.6 %collective-permute-done.32 = bf16[36,1152]{1,0:T(8,128)(2,1)S(1)} collective-permute-done((bf16[36,1152]{1,0:T(8,128)(2,1)S(1)}, bf16[36,1152]{1,0:T(8,128)(2,1)S(1)}, u32[]{:S(2)}, u32[]{:S(2)}) %collective-permute-start.32) | collective-permute-done | bytes 82976 | tf_op jit(solution)/shard_map/ppermute | solution.py:225
  201.0 5.0 %collective-permute-done.33 = bf16[36,1152]{1,0:T(8,128)(2,1)S(1)} collective-permute-done((bf16[36,1152]{1,0:T(8,128)(2,1)S(1)}, bf16[36,1152]{1,0:T(8,128)(2,1)S(1)}, u32[]{:S(2)}, u32[]{:S(2)}) %collective-permute-start.33) | collective-permute-done | bytes 82976 | tf_op jit(solution)/shard_map/ppermute | solution.py:225
  206.1 1.0 collective-permute-start.35
  207.1 1.5 collective-permute-start.36
  208.6 1.1 collective-permute-start.37
  209.6 1.9 convolution_convert_fusion
  212.3 1.7 collective-permute-done.37
  214.7 0.9 reshape.91
  (113 shorter events, 13.8 us)
Async XLA Ops:
  0.6 16.6 %collective-permute-start.1 = (bf16[256,1152]{1,0:T(8,128)(2,1)}, bf16[256,1152]{1,0:T(8,128)(2,1)S(1)}, u32[]{:S(2)}, u32[]{:S(2)}) collective-permute-start(bf16[256,1152]{1,0:T(8,128)(2,1)} %refs_2_.6), channel_id=1, source_target_pairs={{0,16},{8,24},{16,0},{24,8},{1,17},{9,25},{17,1},{25,9},{2,18},{10... | collective-permute-start | bytes 1769480 | tf_op jit(solution)/shard_map/ppermute | solution.py:225
  3.7 15.3 %collective-permute-start = (bf16[256,1152]{1,0:T(8,128)(2,1)}, bf16[256,1152]{1,0:T(8,128)(2,1)S(1)}, u32[]{:S(2)}, u32[]{:S(2)}) collective-permute-start(bf16[256,1152]{1,0:T(8,128)(2,1)} %refs_2_.6), channel_id=1, source_target_pairs={{0,8},{8,0},{16,24},{24,16},{1,9},{9,1},{17,25},{25,17},{2,10},{10... | collective-permute-start | bytes 1769480 | tf_op jit(solution)/shard_map/ppermute | solution.py:225
  11.1 9.6 %copy-start.16 = (bf16[256,1152]{1,0:T(8,128)(2,1)S(1)}, bf16[256,1152]{1,0:T(8,128)(2,1)}, u32[]{:S(2)}) copy-start(bf16[256,1152]{1,0:T(8,128)(2,1)} %refs_2_.6) | copy-start | bytes 1769476
  16.1 20.7 %collective-permute-start.4 = (bf16[368,1152]{1,0:T(8,128)(2,1)}, bf16[368,1152]{1,0:T(8,128)(2,1)S(1)}, u32[]{:S(2)}, u32[]{:S(2)}) collective-permute-start(bf16[368,1152]{1,0:T(8,128)(2,1)} %get-tuple-element.44), channel_id=1, source_target_pairs={{0,1},{1,0},{2,3},{3,2},{4,5},{5,4},{6,7},{7,6},{8,9},{9,8},{10,11... | collective-permute-start | bytes 2543624 | tf_op jit(solution)/shard_map/ppermute | solution.py:225
  17.2 9.5 %copy-start.10 = (bf16[256,1152]{1,0:T(8,128)(2,1)}, bf16[256,1152]{1,0:T(8,128)(2,1)S(1)}, u32[]{:S(2)}) copy-start(bf16[256,1152]{1,0:T(8,128)(2,1)S(1)} %collective-permute-done.1.refs_4_) | copy-start | bytes 1769476
  17.2 8.4 %collective-permute-start.2 = (bf16[128,1152]{1,0:T(8,128)(2,1)S(1)}, bf16[128,1152]{1,0:T(8,128)(2,1)S(1)}, u32[]{:S(2)}, u32[]{:S(2)}) collective-permute-start(bf16[128,1152]{1,0:T(8,128)(2,1)S(1)} %slice.114), channel_id=1, source_target_pairs={{0,8},{8,0},{16,24},{24,16},{1,9},{9,1},{17,25},{25,17},{2,10},{10... | collective-permute-start | bytes 884744 | tf_op jit(solution)/shard_map/ppermute | solution.py:225
  19.0 7.7 %copy-start.11 = (bf16[256,1152]{1,0:T(8,128)(2,1)}, bf16[256,1152]{1,0:T(8,128)(2,1)S(1)}, u32[]{:S(2)}) copy-start(bf16[256,1152]{1,0:T(8,128)(2,1)S(1)} %collective-permute-done.refs_3_) | copy-start | bytes 1769476
  19.0 7.7 %collective-permute-start.3 = (bf16[128,1152]{1,0:T(8,128)(2,1)S(1)}, bf16[128,1152]{1,0:T(8,128)(2,1)S(1)}, u32[]{:S(2)}, u32[]{:S(2)}) collective-permute-start(bf16[128,1152]{1,0:T(8,128)(2,1)S(1)} %slice.115), channel_id=1, source_target_pairs={{0,16},{8,24},{16,0},{24,8},{1,17},{9,25},{17,1},{25,9},{2,18},{10... | collective-permute-start | bytes 884744 | tf_op jit(solution)/shard_map/ppermute | solution.py:225
  20.6 27.2 %collective-permute-start.6 = (bf16[256,1152]{1,0:T(8,128)(2,1)S(1)}, bf16[256,1152]{1,0:T(8,128)(2,1)S(1)}, u32[]{:S(2)}, u32[]{:S(2)}) collective-permute-start(bf16[256,1152]{1,0:T(8,128)(2,1)S(1)} %copy-done.16), channel_id=1, source_target_pairs={{0,4},{1,5},{2,6},{3,7},{4,0},{5,1},{6,2},{7,3},{8,12},{9,13},{10,... | collective-permute-start | bytes 1769480 | tf_op jit(solution)/shard_map/ppermute | solution.py:225
  25.7 1.1 copy-start.23
  26.7 0.7 copy-start.24
  36.9 0.9 copy-start.4
  37.8 26.5 %copy-start.12 = (s32[256]{0:T(256)S(1)}, s32[256]{0:T(256)}, u32[]{:S(2)}) copy-start(s32[256]{0:T(256)} %param.9) | copy-start | bytes 3076
  47.8 14.8 %copy-start.17 = (bf16[256,1152]{1,0:T(8,128)(2,1)}, bf16[256,1152]{1,0:T(8,128)(2,1)S(1)}, u32[]{:S(2)}) copy-start(bf16[256,1152]{1,0:T(8,128)(2,1)S(1)} %collective-permute-done.6.refs_3_) | copy-start | bytes 1769476
  47.8 14.2 %collective-permute-start.7 = (bf16[256,1152]{1,0:T(8,128)(2,1)S(1)}, bf16[256,1152]{1,0:T(8,128)(2,1)S(1)}, u32[]{:S(2)}, u32[]{:S(2)}) collective-permute-start(bf16[256,1152]{1,0:T(8,128)(2,1)S(1)} %collective-permute-done.6.refs_3_), channel_id=1, source_target_pairs={{0,8},{8,0},{16,24},{24,16},{1,9},{9,1},{17,25},{25,17},{2,10},{10... | collective-permute-start | bytes 1769480 | tf_op jit(solution)/shard_map/ppermute | solution.py:225
  48.3 14.2 %collective-permute-start.8 = (bf16[256,1152]{1,0:T(8,128)(2,1)S(1)}, bf16[256,1152]{1,0:T(8,128)(2,1)S(1)}, u32[]{:S(2)}, u32[]{:S(2)}) collective-permute-start(bf16[256,1152]{1,0:T(8,128)(2,1)S(1)} %collective-permute-done.6.refs_3_), channel_id=1, source_target_pairs={{0,16},{8,24},{16,0},{24,8},{1,17},{9,25},{17,1},{25,9},{2,18},{10... | collective-permute-start | bytes 1769480 | tf_op jit(solution)/shard_map/ppermute | solution.py:225
  49.4 36.9 %collective-permute-start.11 = (bf16[368,1152]{1,0:T(8,128)(2,1)}, bf16[368,1152]{1,0:T(8,128)(2,1)S(1)}, u32[]{:S(2)}, u32[]{:S(2)}) collective-permute-start(bf16[368,1152]{1,0:T(8,128)(2,1)} %get-tuple-element.51), channel_id=1, source_target_pairs={{0,2},{1,3},{2,0},{3,1},{4,6},{5,7},{6,4},{7,5},{8,10},{9,11},{10,... | collective-permute-start | bytes 2543624 | tf_op jit(solution)/shard_map/ppermute | solution.py:225
  50.1 36.2 %collective-permute-start.12 = (bf16[368,1152]{1,0:T(8,128)(2,1)}, bf16[368,1152]{1,0:T(8,128)(2,1)S(1)}, u32[]{:S(2)}, u32[]{:S(2)}) collective-permute-start(bf16[368,1152]{1,0:T(8,128)(2,1)} %get-tuple-element.52), channel_id=1, source_target_pairs={{0,3},{1,2},{2,1},{3,0},{4,7},{5,6},{6,5},{7,4},{8,11},{9,10},{10,... | collective-permute-start | bytes 2543624 | tf_op jit(solution)/shard_map/ppermute | solution.py:225
  50.1 14.2 %collective-permute-start.5 = (bf16[176,1152]{1,0:T(8,128)(2,1)}, bf16[176,1152]{1,0:T(8,128)(2,1)}, u32[]{:S(2)}, u32[]{:S(2)}) collective-permute-start(bf16[176,1152]{1,0:T(8,128)(2,1)} %get-tuple-element.47), channel_id=1, source_target_pairs={{0,1},{1,0},{2,3},{3,2},{4,5},{5,4},{6,7},{7,6},{8,9},{9,8},{10,11... | collective-permute-start | bytes 1216520 | tf_op jit(solution)/shard_map/ppermute | solution.py:225
  62.0 7.5 %copy-start.8 = (bf16[256,1152]{1,0:T(8,128)(2,1)}, bf16[256,1152]{1,0:T(8,128)(2,1)S(1)}, u32[]{:S(2)}) copy-start(bf16[256,1152]{1,0:T(8,128)(2,1)S(1)} %collective-permute-done.7.refs_4_) | copy-start | bytes 1769476
  62.0 7.1 %collective-permute-start.10 = (bf16[128,1152]{1,0:T(8,128)(2,1)S(1)}, bf16[128,1152]{1,0:T(8,128)(2,1)}, u32[]{:S(2)}, u32[]{:S(2)}) collective-permute-start(bf16[128,1152]{1,0:T(8,128)(2,1)S(1)} %slice.117), channel_id=1, source_target_pairs={{0,16},{8,24},{16,0},{24,8},{1,17},{9,25},{17,1},{25,9},{2,18},{10... | collective-permute-start | bytes 884744 | tf_op jit(solution)/shard_map/ppermute | solution.py:225
  62.6 6.9 %copy-start.9 = (bf16[256,1152]{1,0:T(8,128)(2,1)}, bf16[256,1152]{1,0:T(8,128)(2,1)S(1)}, u32[]{:S(2)}) copy-start(bf16[256,1152]{1,0:T(8,128)(2,1)S(1)} %collective-permute-done.8.refs_5_) | copy-start | bytes 1769476
  62.6 6.9 %collective-permute-start.9 = (bf16[128,1152]{1,0:T(8,128)(2,1)S(1)}, bf16[128,1152]{1,0:T(8,128)(2,1)}, u32[]{:S(2)}, u32[]{:S(2)}) collective-permute-start(bf16[128,1152]{1,0:T(8,128)(2,1)S(1)} %slice.116), channel_id=1, source_target_pairs={{0,8},{8,0},{16,24},{24,16},{1,9},{9,1},{17,25},{25,17},{2,10},{10... | collective-permute-start | bytes 884744 | tf_op jit(solution)/shard_map/ppermute | solution.py:225
  64.3 22.0 %collective-permute-start.13 = (s32[256]{0:T(256)S(1)}, s32[256]{0:T(256)S(1)}, u32[]{:S(2)}, u32[]{:S(2)}) collective-permute-start(s32[256]{0:T(256)S(1)} %copy-done.12), channel_id=1, source_target_pairs={{0,4},{1,5},{2,6},{3,7},{4,0},{5,1},{6,2},{7,3},{8,12},{9,13},{10,... | collective-permute-start | bytes 3080 | tf_op jit(solution)/shard_map/ppermute | solution.py:225
  86.3 0.6 copy-start.14
  86.3 0.9 copy-start.1
  86.3 1.2 copy-start.2
  107.3 1.4 copy-start.18
  107.3 4.4 %copy-start.20 = (bf16[176,1152]{1,0:T(8,128)(2,1)S(1)}, bf16[176,1152]{1,0:T(8,128)(2,1)}, u32[]{:S(2)}) copy-start(bf16[176,1152]{1,0:T(8,128)(2,1)} %get-tuple-element.64) | copy-start | bytes 1216516
  107.3 8.2 %copy-start.19 = (bf16[176,1152]{1,0:T(8,128)(2,1)S(1)}, bf16[176,1152]{1,0:T(8,128)(2,1)}, u32[]{:S(2)}) copy-start(bf16[176,1152]{1,0:T(8,128)(2,1)} %get-tuple-element.65) | copy-start | bytes 1216516
  108.8 6.8 %collective-permute-start.14 = (bf16[192,1152]{1,0:T(8,128)(2,1)S(1)}, bf16[192,1152]{1,0:T(8,128)(2,1)S(1)}, u32[]{:S(2)}, u32[]{:S(2)}) collective-permute-start(bf16[192,1152]{1,0:T(8,128)(2,1)S(1)} %copy-done.18), channel_id=1, source_target_pairs={{0,1},{1,0},{2,3},{3,2},{4,5},{5,4},{6,7},{7,6},{8,9},{9,8},{10,11... | collective-permute-start | bytes 1327112 | tf_op jit(solution)/shard_map/ppermute | solution.py:225
  109.1 32.4 %collective-permute-start.25 = (bf16[256,1152]{1,0:T(8,128)(2,1)S(1)}, bf16[256,1152]{1,0:T(8,128)(2,1)S(1)}, u32[]{:S(2)}, u32[]{:S(2)}) collective-permute-start(bf16[256,1152]{1,0:T(8,128)(2,1)S(1)} %pad_maximum_fusion.3), channel_id=1, source_target_pairs={{0,16},{8,24},{16,0},{24,8},{1,17},{9,25},{17,1},{25,9},{2,18},{10... | collective-permute-start | bytes 1769480 | tf_op jit(solution)/shard_map/ppermute | solution.py:225
  110.1 32.0 %collective-permute-start.23 = (bf16[256,1152]{1,0:T(8,128)(2,1)S(1)}, bf16[256,1152]{1,0:T(8,128)(2,1)S(1)}, u32[]{:S(2)}, u32[]{:S(2)}) collective-permute-start(bf16[256,1152]{1,0:T(8,128)(2,1)S(1)} %pad_maximum_fusion.2), channel_id=1, source_target_pairs={{0,8},{8,0},{16,24},{24,16},{1,9},{9,1},{17,25},{25,17},{2,10},{10... | collective-permute-start | bytes 1769480 | tf_op jit(solution)/shard_map/ppermute | solution.py:225
  111.7 21.9 %collective-permute-start.17 = (bf16[176,1152]{1,0:T(8,128)(2,1)S(1)}, bf16[176,1152]{1,0:T(8,128)(2,1)S(1)}, u32[]{:S(2)}, u32[]{:S(2)}) collective-permute-start(bf16[176,1152]{1,0:T(8,128)(2,1)S(1)} %copy-done.20), channel_id=1, source_target_pairs={{0,2},{1,3},{2,0},{3,1},{4,6},{5,7},{6,4},{7,5},{8,10},{9,11},{10,... | collective-permute-start | bytes 1216520 | tf_op jit(solution)/shard_map/ppermute | solution.py:225
  115.6 19.1 %collective-permute-start.18 = (bf16[176,1152]{1,0:T(8,128)(2,1)S(1)}, bf16[176,1152]{1,0:T(8,128)(2,1)S(1)}, u32[]{:S(2)}, u32[]{:S(2)}) collective-permute-start(bf16[176,1152]{1,0:T(8,128)(2,1)S(1)} %copy-done.19), channel_id=1, source_target_pairs={{0,3},{1,2},{2,1},{3,0},{4,7},{5,6},{6,5},{7,4},{8,11},{9,10},{10,... | collective-permute-start | bytes 1216520 | tf_op jit(solution)/shard_map/ppermute | solution.py:225
  115.6 0.8 copy-start.7
  132.2 43.2 %collective-permute-start.21 = (bf16[256,1152]{1,0:T(8,128)(2,1)}, bf16[256,1152]{1,0:T(8,128)(2,1)}, u32[]{:S(2)}, u32[]{:S(2)}) collective-permute-start(bf16[256,1152]{1,0:T(8,128)(2,1)} %pad_maximum_fusion.1), channel_id=1, source_target_pairs={{0,16},{8,24},{16,0},{24,8},{1,17},{9,25},{17,1},{25,9},{2,18},{10... | collective-permute-start | bytes 1769480 | tf_op jit(solution)/shard_map/ppermute | solution.py:225
  133.6 2.4 %copy-start.21 = (bf16[176,1152]{1,0:T(8,128)(2,1)}, bf16[176,1152]{1,0:T(8,128)(2,1)S(1)}, u32[]{:S(2)}) copy-start(bf16[176,1152]{1,0:T(8,128)(2,1)S(1)} %collective-permute-done.17.refs_3_) | copy-start | bytes 1216516
  133.6 34.4 %collective-permute-start.19 = (bf16[256,1152]{1,0:T(8,128)(2,1)}, bf16[256,1152]{1,0:T(8,128)(2,1)S(1)}, u32[]{:S(2)}, u32[]{:S(2)}) collective-permute-start(bf16[256,1152]{1,0:T(8,128)(2,1)} %pad_maximum_fusion), channel_id=1, source_target_pairs={{0,8},{8,0},{16,24},{24,16},{1,9},{9,1},{17,25},{25,17},{2,10},{10... | collective-permute-start | bytes 1769480 | tf_op jit(solution)/shard_map/ppermute | solution.py:225
  134.7 1.3 copy-start.22
  134.7 24.7 %collective-permute-start.15 = (bf16[192,1152]{1,0:T(8,128)(2,1)}, bf16[192,1152]{1,0:T(8,128)(2,1)}, u32[]{:S(2)}, u32[]{:S(2)}) collective-permute-start(bf16[192,1152]{1,0:T(8,128)(2,1)} %get-tuple-element.61), channel_id=1, source_target_pairs={{0,2},{1,3},{2,0},{3,1},{4,6},{5,7},{6,4},{7,5},{8,10},{9,11},{10,... | collective-permute-start | bytes 1327112 | tf_op jit(solution)/shard_map/ppermute | solution.py:225
  135.9 6.2 %copy-start = (bf16[1024,1152]{1,0:T(8,128)(2,1)S(1)}, bf16[1024,1152]{1,0:T(8,128)(2,1)}, u32[]{:S(2)}) copy-start(bf16[1024,1152]{1,0:T(8,128)(2,1)} %caption_grad.2.refs_1_) | copy-start | bytes 7077892
  141.5 12.6 %copy-start.5 = (bf16[256,1152]{1,0:T(8,128)(2,1)}, bf16[256,1152]{1,0:T(8,128)(2,1)S(1)}, u32[]{:S(2)}) copy-start(bf16[256,1152]{1,0:T(8,128)(2,1)S(1)} %collective-permute-done.25) | copy-start | bytes 1769476
  141.5 17.8 %collective-permute-start.16 = (bf16[192,1152]{1,0:T(8,128)(2,1)}, bf16[192,1152]{1,0:T(8,128)(2,1)}, u32[]{:S(2)}, u32[]{:S(2)}) collective-permute-start(bf16[192,1152]{1,0:T(8,128)(2,1)} %get-tuple-element.62), channel_id=1, source_target_pairs={{0,3},{1,2},{2,1},{3,0},{4,7},{5,6},{6,5},{7,4},{8,11},{9,10},{10,... | collective-permute-start | bytes 1327112 | tf_op jit(solution)/shard_map/ppermute | solution.py:225
  142.2 11.9 %collective-permute-start.24 = (bf16[128,1152]{1,0:T(8,128)(2,1)S(1)}, bf16[128,1152]{1,0:T(8,128)(2,1)S(1)}, u32[]{:S(2)}, u32[]{:S(2)}) collective-permute-start(bf16[128,1152]{1,0:T(8,128)(2,1)S(1)} %fusion.10), channel_id=1, source_target_pairs={{0,16},{8,24},{16,0},{24,8},{1,17},{9,25},{17,1},{25,9},{2,18},{10... | collective-permute-start | bytes 884744 | tf_op jit(solution)/shard_map/ppermute | solution.py:225
  143.2 12.3 %copy-start.3 = (bf16[1024,1152]{1,0:T(8,128)(2,1)S(1)}, bf16[1024,1152]{1,0:T(8,128)(2,1)}, u32[]{:S(2)}) copy-start(bf16[1024,1152]{1,0:T(8,128)(2,1)} %caption_grad.3) | copy-start | bytes 7077892
  143.2 12.4 %copy-start.25 = (bf16[1152,1024]{1,0:T(8,128)(2,1)S(1)}, bf16[1152,1024]{1,0:T(8,128)(2,1)}, u32[]{:S(2)}) copy-start(bf16[1152,1024]{1,0:T(8,128)(2,1)} %get-tuple-element.73) | copy-start | bytes 7077892
  155.0 11.4 %collective-permute-start.26 = (bf16[128,1152]{1,0:T(8,128)(2,1)}, bf16[128,1152]{1,0:T(8,128)(2,1)}, u32[]{:S(2)}, u32[]{:S(2)}) collective-permute-start(bf16[128,1152]{1,0:T(8,128)(2,1)} %get-tuple-element.81), channel_id=1, source_target_pairs={{0,8},{8,0},{16,24},{24,16},{1,9},{9,1},{17,25},{25,17},{2,10},{10... | collective-permute-start | bytes 884744 | tf_op jit(solution)/shard_map/ppermute | solution.py:225
  166.6 0.7 copy-start.13
  166.7 2.5 %copy-start.6 = (bf16[256,1152]{1,0:T(8,128)(2,1)S(1)}, bf16[256,1152]{1,0:T(8,128)(2,1)}, u32[]{:S(2)}) copy-start(bf16[256,1152]{1,0:T(8,128)(2,1)} %copy-done.5) | copy-start | bytes 1769476
  167.2 4.6 %collective-permute-start.28 = (bf16[4,144,1152]{2,0,1:T(4,128)(2,1)S(1)}, bf16[4,144,1152]{2,0,1:T(4,128)(2,1)S(1)}, u32[]{:S(2)}, u32[]{:S(2)}) collective-permute-start(bf16[4,144,1152]{2,0,1:T(4,128)(2,1)S(1)} %bitcast.121), channel_id=1, source_target_pairs={{0,1},{1,0},{2,3},{3,2},{4,5},{5,4},{6,7},{7,6},{8,9},{9,8},{10,11... | collective-permute-start | bytes 3981320 | tf_op jit(solution)/shard_map/ppermute | solution.py:225
  168.0 9.9 %collective-permute-start.20 = (bf16[128,1152]{1,0:T(8,128)(2,1)S(1)}, bf16[128,1152]{1,0:T(8,128)(2,1)S(1)}, u32[]{:S(2)}, u32[]{:S(2)}) collective-permute-start(bf16[128,1152]{1,0:T(8,128)(2,1)S(1)} %fusion.15), channel_id=1, source_target_pairs={{0,16},{8,24},{16,0},{24,8},{1,17},{9,25},{17,1},{25,9},{2,18},{10... | collective-permute-start | bytes 884744 | tf_op jit(solution)/shard_map/ppermute | solution.py:225
  170.3 39.4 %collective-permute-start.27 = (bf16[256,1152]{1,0:T(8,128)(2,1)S(1)}, bf16[256,1152]{1,0:T(8,128)(2,1)S(1)}, u32[]{:S(2)}, u32[]{:S(2)}) collective-permute-start(bf16[256,1152]{1,0:T(8,128)(2,1)S(1)} %pad_maximum_fusion.4), channel_id=1, source_target_pairs={{0,4},{1,5},{2,6},{3,7},{4,0},{5,1},{6,2},{7,3},{8,12},{9,13},{10,... | collective-permute-start | bytes 1769480 | tf_op jit(solution)/shard_map/ppermute | solution.py:225
  172.8 10.7 %collective-permute-start.29 = (bf16[4,36,1152]{2,0,1:T(4,128)(2,1)S(1)}, bf16[4,36,1152]{2,0,1:T(4,128)(2,1)S(1)}, u32[]{:S(2)}, u32[]{:S(2)}) collective-permute-start(bf16[4,36,1152]{2,0,1:T(4,128)(2,1)S(1)} %get-tuple-element.92), channel_id=1, source_target_pairs={{0,8},{8,0},{16,24},{24,16},{1,9},{9,1},{17,25},{25,17},{2,10},{10... | collective-permute-start | bytes 995336 | tf_op jit(solution)/shard_map/ppermute | solution.py:225
  173.8 17.8 %collective-permute-start.30 = (bf16[4,36,1152]{2,0,1:T(4,128)(2,1)S(1)}, bf16[4,36,1152]{2,0,1:T(4,128)(2,1)S(1)}, u32[]{:S(2)}, u32[]{:S(2)}) collective-permute-start(bf16[4,36,1152]{2,0,1:T(4,128)(2,1)S(1)} %get-tuple-element.94), channel_id=1, source_target_pairs={{0,16},{8,24},{16,0},{24,8},{1,17},{9,25},{17,1},{25,9},{2,18},{10... | collective-permute-start | bytes 995336 | tf_op jit(solution)/shard_map/ppermute | solution.py:225
  175.3 16.3 %collective-permute-start.31 = (bf16[4,36,1152]{2,0,1:T(4,128)(2,1)S(1)}, bf16[4,36,1152]{2,0,1:T(4,128)(2,1)S(1)}, u32[]{:S(2)}, u32[]{:S(2)}) collective-permute-start(bf16[4,36,1152]{2,0,1:T(4,128)(2,1)S(1)} %get-tuple-element.93), channel_id=1, source_target_pairs={{0,24},{8,16},{16,8},{24,0},{1,25},{9,17},{17,9},{25,1},{2,26},{10... | collective-permute-start | bytes 995336 | tf_op jit(solution)/shard_map/ppermute | solution.py:225
  179.0 18.3 %collective-permute-start.22 = (bf16[128,1152]{1,0:T(8,128)(2,1)S(1)}, bf16[128,1152]{1,0:T(8,128)(2,1)S(1)}, u32[]{:S(2)}, u32[]{:S(2)}) collective-permute-start(bf16[128,1152]{1,0:T(8,128)(2,1)S(1)} %get-tuple-element.87), channel_id=1, source_target_pairs={{0,8},{8,0},{16,24},{24,16},{1,9},{9,1},{17,25},{25,17},{2,10},{10... | collective-permute-start | bytes 884744 | tf_op jit(solution)/shard_map/ppermute | solution.py:225
  192.0 17.7 %copy-start.15 = (bf16[1152,1152]{1,0:T(8,128)(2,1)S(1)}, bf16[1152,1152]{1,0:T(8,128)(2,1)}, u32[]{:S(2)}) copy-start(bf16[1152,1152]{1,0:T(8,128)(2,1)} %refs_2_.7) | copy-start | bytes 7962628
  192.7 8.3 %collective-permute-start.32 = (bf16[36,1152]{1,0:T(8,128)(2,1)S(1)}, bf16[36,1152]{1,0:T(8,128)(2,1)S(1)}, u32[]{:S(2)}, u32[]{:S(2)}) collective-permute-start(bf16[36,1152]{1,0:T(8,128)(2,1)S(1)} %bitcast.124), channel_id=1, source_target_pairs={{0,2},{1,3},{2,0},{3,1},{4,6},{5,7},{6,4},{7,5},{8,10},{9,11},{10,... | collective-permute-start | bytes 248840 | tf_op jit(solution)/shard_map/ppermute | solution.py:225
  194.7 11.3 %collective-permute-start.33 = (bf16[36,1152]{1,0:T(8,128)(2,1)S(1)}, bf16[36,1152]{1,0:T(8,128)(2,1)S(1)}, u32[]{:S(2)}, u32[]{:S(2)}) collective-permute-start(bf16[36,1152]{1,0:T(8,128)(2,1)S(1)} %bitcast.126), channel_id=1, source_target_pairs={{0,4},{1,5},{2,6},{3,7},{4,0},{5,1},{6,2},{7,3},{8,12},{9,13},{10,... | collective-permute-start | bytes 248840 | tf_op jit(solution)/shard_map/ppermute | solution.py:225
  195.7 10.3 %collective-permute-start.34 = (bf16[36,1152]{1,0:T(8,128)(2,1)S(1)}, bf16[36,1152]{1,0:T(8,128)(2,1)S(1)}, u32[]{:S(2)}, u32[]{:S(2)}) collective-permute-start(bf16[36,1152]{1,0:T(8,128)(2,1)S(1)} %bitcast.128), channel_id=1, source_target_pairs={{0,6},{1,7},{2,4},{3,5},{4,2},{5,3},{6,0},{7,1},{8,14},{9,15},{10,... | collective-permute-start | bytes 248840 | tf_op jit(solution)/shard_map/ppermute | solution.py:225
  206.1 5.5 %collective-permute-start.35 = (bf16[36,1152]{1,0:T(8,128)(2,1)S(1)}, bf16[36,1152]{1,0:T(8,128)(2,1)S(1)}, u32[]{:S(2)}, u32[]{:S(2)}) collective-permute-start(bf16[36,1152]{1,0:T(8,128)(2,1)S(1)} %fusion.19), channel_id=1, source_target_pairs={{0,8},{8,0},{16,24},{24,16},{1,9},{9,1},{17,25},{25,17},{2,10},{10... | collective-permute-start | bytes 248840 | tf_op jit(solution)/shard_map/ppermute | solution.py:225
  207.1 5.2 %collective-permute-start.36 = (bf16[36,1152]{1,0:T(8,128)(2,1)S(1)}, bf16[36,1152]{1,0:T(8,128)(2,1)S(1)}, u32[]{:S(2)}, u32[]{:S(2)}) collective-permute-start(bf16[36,1152]{1,0:T(8,128)(2,1)S(1)} %fusion.19), channel_id=1, source_target_pairs={{0,16},{8,24},{16,0},{24,8},{1,17},{9,25},{17,1},{25,9},{2,18},{10... | collective-permute-start | bytes 248840 | tf_op jit(solution)/shard_map/ppermute | solution.py:225
  208.6 5.5 %collective-permute-start.37 = (bf16[36,1152]{1,0:T(8,128)(2,1)S(1)}, bf16[36,1152]{1,0:T(8,128)(2,1)S(1)}, u32[]{:S(2)}, u32[]{:S(2)}) collective-permute-start(bf16[36,1152]{1,0:T(8,128)(2,1)S(1)} %fusion.19), channel_id=1, source_target_pairs={{0,24},{8,16},{16,8},{24,0},{1,25},{9,17},{17,9},{25,1},{2,26},{10... | collective-permute-start | bytes 248840 | tf_op jit(solution)/shard_map/ppermute | solution.py:225
